TPU v7x, 32 devices: a whole 2x2x4 slice. The times are simulated.
32 devices in a mesh: sub: 4 (over z), rng: 8 (over y, x, core).
Axes of the slice: x: 2, y: 2, z: 4, core: 2. Of those that a mesh axis runs over, the one named last changes fastest.
Arguments:
- echoes: bfloat16 [2, 2048, 4096], P(None, 'sub', 'rng'), may hold values from -6 to 6
- chirp: bfloat16 [2, 512], replicated, may hold values from -0.1875 to 0.1875
- offsets: int32 [2, 4, 2, 512], P(None, 'sub'), may hold values from 0 to 504
- weights: bfloat16 [2, 4, 2, 2, 512, 8], P(None, 'sub'), may hold values from -1 to 1
- owners: int32 [4, 8, 512, 1], P('sub', 'rng'), may hold values from 0 to 31; in each aligned block of 512 rows (0 to 511, 512 to 1023, ..., all dimensions but the last counted through in order) at most 32 rows name the same one
- targets: int32 [4, 8, 512], P('sub', 'rng'), may hold values from 0 to 511
Outputs:
- tiles: bfloat16 [2, 2048, 4096], P(None, 'sub', 'rng')
Inputs may be any that keep to these rules, and one draw needn't show every extreme that they name: `owners`: within the 512 rows of one device, no tile is named more than 32 times, a bound that some block reaches.
All inputs are finite; a program needn't handle non-finite values.
Results may differ from a plain program's by a relative error of at most 0.0069.
Values may be sent and summed in bfloat16 or wider, within the bound.
A program may use at most 384 MiB of HBM per device.

v0:
```python
import jax
import jax.numpy as jnp
from jax import lax
from jax.sharding import PartitionSpec as P

RBLK = 512


def shifted(value, axis, steps):
    count = lax.axis_size(axis)
    first, last = (max(0, -steps), min(count, count - steps))
    return lax.ppermute(value, axis, [(source, source + steps) for source in range(first, last)])


def from_partner(value, axis, apart):
    return lax.ppermute(value, axis, [(i, i ^ 1 << apart) for i in range(lax.axis_size(axis))])


def replica_matrix(chirp, block_len):
    taps_len = chirp.shape[1]
    width = block_len + taps_len
    parts = []
    for part in range(2):
        padded = jnp.concatenate([chirp[part], jnp.zeros((width + 1 - taps_len,), chirp.dtype)])
        tiled = jnp.tile(padded, block_len)[: block_len * width].reshape(block_len, width)
        parts.append(tiled.T)
    h_real, h_imag = (parts[0], parts[1])
    upper = jnp.concatenate([h_real, -h_imag], axis=1)
    lower = jnp.concatenate([h_imag, h_real], axis=1)
    return jnp.concatenate([upper, lower], axis=0)


def merge_matrix(starts, kernel):
    beams = starts.shape[0]
    taps_len = kernel.shape[-1]
    spots = starts[:, None] + jnp.arange(taps_len, dtype=jnp.int32)[None, :]
    hit = (spots[:, :, None] == jnp.arange(beams, dtype=jnp.int32)[None, None, :]).astype(
        jnp.float32
    )
    g_real = jnp.einsum("bk,bks->bs", kernel[0].astype(jnp.float32), hit).astype(jnp.bfloat16)
    g_imag = jnp.einsum("bk,bks->bs", kernel[1].astype(jnp.float32), hit).astype(jnp.bfloat16)
    upper = jnp.concatenate([g_real, -g_imag], axis=1)
    lower = jnp.concatenate([g_imag, g_real], axis=1)
    return jnp.concatenate([upper, lower], axis=0)


def group_slots(dest, devices):
    onehot = (dest[:, None] == jnp.arange(devices, dtype=jnp.int32)[None, :]).astype(jnp.int32)
    return jnp.sum((jnp.cumsum(onehot, axis=0) - 1) * onehot, axis=1)


def route_rows(send, labels):
    got, marks = (
        lax.all_to_all(send, ("sub", "rng"), split_axis=0, concat_axis=0, tiled=True),
        lax.all_to_all(labels, ("sub", "rng"), split_axis=0, concat_axis=0, tiled=True),
    )
    return (got, marks)


def on_device(echoes, chirp, offsets, weights, owners, targets):
    p_dev = echoes.shape[1]
    r_dev = echoes.shape[2]
    n_sub = lax.axis_size("sub")
    n_rng = lax.axis_size("rng")
    devices = n_sub * n_rng
    capacity = max(2, 2 * p_dev // devices)
    tail = shifted(echoes, "rng", -1)
    extended = jnp.concatenate([echoes, tail], axis=2)
    matrix = replica_matrix(chirp, RBLK)
    stacked = jnp.concatenate([extended[0], extended[1]], axis=1)
    block_out = jnp.dot(stacked, matrix, preferred_element_type=jnp.float32).astype(jnp.bfloat16)
    pieces = block_out.reshape(p_dev, 2, RBLK)
    image = pieces.transpose(1, 0, 2).reshape(2 * p_dev, r_dev)
    section_count = offsets.shape[0]
    for section in range(section_count):
        partner = from_partner(image, "sub", section)
        mine = merge_matrix(offsets[section, 0, 0], weights[section, 0, 0])
        theirs = merge_matrix(offsets[section, 0, 1], weights[section, 0, 1])
        merged = jnp.dot(mine, image, preferred_element_type=jnp.float32)
        merged = merged + jnp.dot(theirs, partner, preferred_element_type=jnp.float32)
        image = merged.astype(jnp.bfloat16)
    rows = image.reshape(2, p_dev, r_dev).transpose(1, 0, 2).reshape(p_dev, 2 * r_dev)
    dest = owners.reshape(p_dev)
    aim = targets.reshape(p_dev)
    slot = dest * capacity + group_slots(dest, devices)
    pick = jnp.arange(devices * capacity, dtype=jnp.int32)[:, None] == slot[None, :]
    send = jnp.dot(pick.astype(jnp.bfloat16), rows, preferred_element_type=jnp.float32).astype(
        jnp.bfloat16
    )
    labels = jnp.sum(jnp.where(pick, aim[None, :] + 1, 0), axis=1) - 1
    got, marks = route_rows(
        send.reshape(devices, capacity, 2 * r_dev), labels.reshape(devices, capacity)
    )
    got_flat = got.reshape(devices * capacity, 2 * r_dev)
    mark_flat = marks.reshape(devices * capacity)
    place = (jnp.arange(p_dev, dtype=jnp.int32)[:, None] == mark_flat[None, :]).astype(jnp.bfloat16)
    tile = jnp.dot(place, got_flat, preferred_element_type=jnp.float32).astype(jnp.bfloat16)
    return tile.reshape(p_dev, 2, r_dev).transpose(1, 0, 2)


def solution(mesh):
    in_specs = (
        P(None, "sub", "rng"),
        P(),
        P(None, "sub", None, None),
        P(None, "sub", None, None, None, None),
        P("sub", "rng", None, None),
        P("sub", "rng", None),
    )
    out_specs = P(None, "sub", "rng")
    return jax.shard_map(
        on_device, mesh=mesh, in_specs=in_specs, out_specs=out_specs, check_vma=False
    )
```

profile of v0, /device:TPU:1, one launch (start us, length us, event | category | flops | bytes accessed | tf_op | source)
XLA Modules:
  0.0 183.5 jit_solution(4830059943614350151)
XLA Ops:
  0.0 2.0 %collective-permute-start = (bf16[2,512,512]{2,1,0:T(8,128)(2,1)}, bf16[2,512,512]{2,1,0:T(8,128)(2,1)}, u32[]{:S(2)}, u32[]{:S(2)}) collective-permute-start(bf16[2,512,512]{2,1,0:T(8,128)(2,1)} %param.6), channel_id=1, source_target_pairs={{1,0},{2,1},{3,2},{4,3},{5,4},{6,5},{7,6},{9,8},{10,9},{11,10},{12... | collective-permute-start | bytes 3145736 | tf_op jit(solution)/shard_map/ppermute | solution.py:12
  7.2 8.2 %all-to-all-start = ((s32[32,1,32]{2,1,0:T(1,128)}), s32[32,1,32]{2,1,0:T(1,128)}, u32[]{:S(2)}, u32[]{:S(2)}) async-start(s32[32,1,32]{2,1,0:T(1,128)} %sub.18), calls=%async_computation | async-start | bytes 32768 | tf_op jit(solution)/shard_map/all_to_all | solution.py:55
  15.4 1.3 slice_reduce_fusion.1
  20.8 2.2 %fusion.4 = bf16[512,1,512]{2,1,0:T(2,128)(2,1)S(1)} fusion(bf16[512,8,1]{1,2,0:T(2,128)(2,1)S(1)} %copy.22, s32[512,8]{1,0:T(8,128)S(1)} %iota_add_fusion.2), kind=kOutput, calls=%fused_computation.7 | convolution fusion | flops 6291456 | bytes 548864 | tf_op jit(solution)/shard_map/bk,bks->bs/dot_general | solution.py:41
  24.5 2.2 %fusion.2 = bf16[512,1,512]{2,1,0:T(2,128)(2,1)S(1)} fusion(bf16[512,8,1]{1,2,0:T(2,128)(2,1)S(1)} %copy.26, s32[512,8]{1,0:T(8,128)S(1)} %iota_add_fusion.1), kind=kOutput, calls=%fused_computation.4 | convolution fusion | flops 6291456 | bytes 548864 | tf_op jit(solution)/shard_map/bk,bks->bs/dot_general | solution.py:41
  32.3 2.2 %fusion.5 = bf16[512,1,512]{2,1,0:T(2,128)(2,1)S(1)} fusion(bf16[512,8,1]{1,2,0:T(2,128)(2,1)S(1)} %copy.20, s32[512,8]{1,0:T(8,128)S(1)} %copy-done.11), kind=kOutput, calls=%fused_computation.8 | convolution fusion | flops 6291456 | bytes 548864 | tf_op jit(solution)/shard_map/bk,bks->bs/dot_general | solution.py:40
  34.5 2.2 %fusion.3 = bf16[512,1,512]{2,1,0:T(2,128)(2,1)S(1)} fusion(bf16[512,8,1]{1,2,0:T(2,128)(2,1)S(1)} %copy.24, s32[512,8]{1,0:T(8,128)S(1)} %copy-done.13), kind=kOutput, calls=%fused_computation.5 | convolution fusion | flops 6291456 | bytes 548864 | tf_op jit(solution)/shard_map/bk,bks->bs/dot_general | solution.py:40
  36.8 2.2 %fusion.7 = bf16[512,1,512]{2,1,0:T(2,128)(2,1)S(1)} fusion(bf16[512,8,1]{1,2,0:T(2,128)(2,1)S(1)} %copy-done.14, s32[512,8]{1,0:T(8,128)S(1)} %iota_add_fusion.3), kind=kOutput, calls=%fused_computation.11 | convolution fusion | flops 6291456 | bytes 548864 | tf_op jit(solution)/shard_map/bk,bks->bs/dot_general | solution.py:40
  39.1 1.4 constant_dynamic-update-slice_fusion
  42.0 2.4 %fusion.66 = bf16[512,1024]{1,0:T(8,128)(2,1)S(1)} fusion(bf16[1024,512]{0,1:T(8,128)(2,1)S(1)} %bitcast.121, bf16[1024,512]{0,1:T(8,128)(2,1)S(1)} %bitcast.119, bf16[1024,512]{0,1:T(8,128)(2,1)S(1)} %copy-done.1, bf16[512,1024]{1,0:T(8,128)(2,1)S(1)} %get-tuple-element.16, bf16[512,1024]{1,0:T(8,128)(2,1)S(1)} %get-tuple-element.15), kind=kOutput, calls=%fused_computation.71 | convolution fusion | flops 2168979456 | bytes 6291456 | tf_op jit(solution)/shard_map/dot_general | solution.py:71
  44.5 1.5 collective-permute-start.1
  48.9 2.2 %fusion.6 = bf16[512,1,512]{2,1,0:T(2,128)(2,1)S(1)} fusion(bf16[512,8,1]{1,2,0:T(2,128)(2,1)S(1)} %copy.18, s32[512,8]{1,0:T(8,128)S(1)} %iota_add_fusion.3), kind=kOutput, calls=%fused_computation.10 | convolution fusion | flops 6291456 | bytes 548864 | tf_op jit(solution)/shard_map/bk,bks->bs/dot_general | solution.py:41
  51.2 2.4 %fusion.1 = bf16[512,1,512]{2,1,0:T(2,128)(2,1)S(1)} fusion(bf16[512,8,1]{1,2,0:T(2,128)(2,1)S(1)} %copy-done.15, s32[512,8]{1,0:T(8,128)S(1)} %copy-done.8), kind=kOutput, calls=%fused_computation.2 | convolution fusion | flops 6291456 | bytes 548864 | tf_op jit(solution)/shard_map/bk,bks->bs/dot_general | solution.py:40
  54.9 14.2 %collective-permute-done.1 = bf16[1024,512]{1,0:T(8,128)(2,1)} collective-permute-done((bf16[1024,512]{1,0:T(8,128)(2,1)S(1)}, bf16[1024,512]{1,0:T(8,128)(2,1)}, u32[]{:S(2)}, u32[]{:S(2)}) %collective-permute-start.1) | collective-permute-done | bytes 1048608 | tf_op jit(solution)/shard_map/ppermute | solution.py:16
  69.1 3.4 %add_convert_fusion.1 = bf16[1024,512]{1,0:T(8,128)(2,1)} fusion(f32[1024,512]{1,0:T(8,128)S(1)} %fusion.32, bf16[1024,512]{1,0:T(8,128)(2,1)} %collective-permute-done.1, bf16[512,512]{1,0:T(8,128)(2,1)S(1)} %bitcast.129, bf16[512,512]{1,0:T(8,128)(2,1)S(1)} %copy-done.7, bf16[512,512]{1,0:T(8,128)(2,1)S(1)} %copy-done.6), kind=kOutput, calls=%fused_computation.64 | convolution fusion | flops 1083179008 | bytes 5767168 | tf_op jit(solution)/shard_map/dot_general | solution.py:80
  72.5 2.2 %collective-permute-start.2 = (bf16[1024,512]{1,0:T(8,128)(2,1)}, bf16[1024,512]{1,0:T(8,128)(2,1)}, u32[]{:S(2)}, u32[]{:S(2)}) collective-permute-start(bf16[1024,512]{1,0:T(8,128)(2,1)} %add_convert_fusion.1), channel_id=1, source_target_pairs={{0,16},{8,24},{16,0},{24,8},{1,17},{9,25},{17,1},{25,9},{2,18},{10... | collective-permute-start | bytes 3145736 | tf_op jit(solution)/shard_map/ppermute | solution.py:16
  75.8 2.2 %fusion = bf16[512,1,512]{2,1,0:T(2,128)(2,1)S(1)} fusion(bf16[512,8,1]{1,2,0:T(2,128)(2,1)S(1)} %copy.30, s32[512,8]{1,0:T(8,128)S(1)} %copy-done.9), kind=kOutput, calls=%fused_computation.1 | convolution fusion | flops 6291456 | bytes 548864 | tf_op jit(solution)/shard_map/bk,bks->bs/dot_general | solution.py:41
  78.1 2.5 %fusion.24 = f32[1024,512]{1,0:T(8,128)S(1)} fusion(bf16[1024,512]{1,0:T(8,128)(2,1)} %add_convert_fusion.1, bf16[512,512]{1,0:T(8,128)(2,1)S(1)} %bitcast.131, bf16[512,512]{1,0:T(8,128)(2,1)S(1)} %get-tuple-element.10, bf16[512,512]{1,0:T(8,128)(2,1)S(1)} %get-tuple-element.9), kind=kOutput, calls=%fused_computation.28 | convolution fusion | flops 1082130432 | bytes 4718592 | tf_op jit(solution)/shard_map/dot_general | solution.py:79
  80.6 39.6 %collective-permute-done.2 = bf16[1024,512]{1,0:T(8,128)(2,1)} collective-permute-done((bf16[1024,512]{1,0:T(8,128)(2,1)}, bf16[1024,512]{1,0:T(8,128)(2,1)}, u32[]{:S(2)}, u32[]{:S(2)}) %collective-permute-start.2) | collective-permute-done | bytes 1048608 | tf_op jit(solution)/shard_map/ppermute | solution.py:16
  120.1 2.5 %add_convert_fusion = bf16[1024,512]{1,0:T(8,128)(2,1)S(1)} fusion(f32[1024,512]{1,0:T(8,128)S(1)} %fusion.24, bf16[1024,512]{1,0:T(8,128)(2,1)} %collective-permute-done.2, bf16[512,512]{1,0:T(8,128)(2,1)S(1)} %bitcast.130, bf16[512,512]{1,0:T(8,128)(2,1)S(1)} %get-tuple-element.8, bf16[512,512]{1,0:T(8,128)(2,1)S(1)} %get-tuple-element.7), kind=kOutput, calls=%fused_computation.63 | convolution fusion | flops 1083179008 | bytes 5767168 | tf_op jit(solution)/shard_map/dot_general | solution.py:80
  123.3 2.6 %fusion.61 = bf16[1024,1024]{1,0:T(8,128)(2,1)} fusion(bf16[512,1024]{0,1:T(8,128)(2,1)S(1)} %bitcast.127, s32[512]{0:T(512)S(1)} %copy-done.24), kind=kOutput, calls=%fused_computation.70 | convolution fusion | flops 1075314688 | bytes 3147776 | tf_op jit(solution)/shard_map/dot_general | solution.py:87
  125.9 7.0 %all-to-all-start.1 = ((bf16[32,32,1024]{2,1,0:T(8,128)(2,1)}), bf16[32,32,1024]{2,1,0:T(8,128)(2,1)S(1)}, u32[]{:S(2)}, u32[]{:S(2)}) async-start(bf16[32,32,1024]{2,1,0:T(8,128)(2,1)} %bitcast.42), calls=%async_computation.1 | async-start | bytes 4194304 | tf_op jit(solution)/shard_map/all_to_all | solution.py:54
  133.4 1.4 reduce.9
  134.9 46.3 %all-to-all-done.1 = bf16[32,32,1024]{2,1,0:T(8,128)(2,1)S(1)} async-done(((bf16[32,32,1024]{2,1,0:T(8,128)(2,1)}), bf16[32,32,1024]{2,1,0:T(8,128)(2,1)S(1)}, u32[]{:S(2)}, u32[]{:S(2)}) %all-to-all-start.1) | async-done | bytes 2097184 | tf_op jit(solution)/shard_map/all_to_all | solution.py:54
  (107 shorter events, 26.4 us)
Async XLA Ops:
  0.0 39.1 %collective-permute-start = (bf16[2,512,512]{2,1,0:T(8,128)(2,1)}, bf16[2,512,512]{2,1,0:T(8,128)(2,1)}, u32[]{:S(2)}, u32[]{:S(2)}) collective-permute-start(bf16[2,512,512]{2,1,0:T(8,128)(2,1)} %param.6), channel_id=1, source_target_pairs={{1,0},{2,1},{3,2},{4,3},{5,4},{6,5},{7,6},{9,8},{10,9},{11,10},{12... | collective-permute-start | bytes 3145736 | tf_op jit(solution)/shard_map/ppermute | solution.py:12
  7.2 118.7 %all-to-all-start = ((s32[32,1,32]{2,1,0:T(1,128)}), s32[32,1,32]{2,1,0:T(1,128)}, u32[]{:S(2)}, u32[]{:S(2)}) async-start(s32[32,1,32]{2,1,0:T(1,128)} %sub.18), calls=%async_computation | async-start | bytes 32768 | tf_op jit(solution)/shard_map/all_to_all | solution.py:55
  18.3 1.6 copy-start.16
  18.3 2.2 %copy-start.22 = (s32[2,1,2,512]{3,2,1,0:T(2,128)S(1)}, s32[2,1,2,512]{3,2,1,0:T(2,128)}, u32[]{:S(2)}) copy-start(s32[2,1,2,512]{3,2,1,0:T(2,128)} %param.8) | copy-start | bytes 24580
  20.7 2.4 %copy-start.10 = (s32[512,8]{1,0:T(8,128)}, s32[512,8]{1,0:T(8,128)S(1)}, u32[]{:S(2)}) copy-start(s32[512,8]{1,0:T(8,128)S(1)} %iota_add_fusion.2) | copy-start | bytes 49156
  24.3 2.4 %copy-start.12 = (s32[512,8]{1,0:T(8,128)}, s32[512,8]{1,0:T(8,128)S(1)}, u32[]{:S(2)}) copy-start(s32[512,8]{1,0:T(8,128)S(1)} %iota_add_fusion.1) | copy-start | bytes 49156
  29.5 1.5 copy-start.20
  29.6 1.7 copy-start.19
  29.6 2.5 %copy-start = (bf16[2,512,512]{2,1,0:T(8,128)(2,1)S(1)}, bf16[2,512,512]{2,1,0:T(8,128)(2,1)}, u32[]{:S(2)}) copy-start(bf16[2,512,512]{2,1,0:T(8,128)(2,1)} %param.6) | copy-start | bytes 3145732
  32.3 2.3 %copy-start.13 = (s32[512,8]{1,0:T(8,128)S(1)}, s32[512,8]{1,0:T(8,128)}, u32[]{:S(2)}) copy-start(s32[512,8]{1,0:T(8,128)} %copy-done.12) | copy-start | bytes 49156
  34.5 2.3 %copy-start.14 = (bf16[512,8,1]{1,2,0:T(2,128)(2,1)S(1)}, bf16[512,8,1]{1,2,0:T(2,128)(2,1)}, u32[]{:S(2)}) copy-start(bf16[512,8,1]{1,2,0:T(2,128)(2,1)} %copy.16) | copy-start | bytes 24580
  40.5 1.5 copy-start.2
  44.5 3.4 %copy-start.18 = (bf16[512,8,1]{0,1,2:T(8,128)(2,1)S(1)}, bf16[512,8,1]{0,1,2:T(8,128)(2,1)}, u32[]{:S(2)}) copy-start(bf16[512,8,1]{0,1,2:T(8,128)(2,1)} %get-tuple-element.22) | copy-start | bytes 24580
  44.5 3.5 %copy-start.17 = (bf16[512,8,1]{0,1,2:T(8,128)(2,1)S(1)}, bf16[512,8,1]{0,1,2:T(8,128)(2,1)}, u32[]{:S(2)}) copy-start(bf16[512,8,1]{0,1,2:T(8,128)(2,1)} %get-tuple-element.24) | copy-start | bytes 24580
  44.5 24.6 %collective-permute-start.1 = (bf16[1024,512]{1,0:T(8,128)(2,1)S(1)}, bf16[1024,512]{1,0:T(8,128)(2,1)}, u32[]{:S(2)}, u32[]{:S(2)}) collective-permute-start(bf16[1024,512]{1,0:T(8,128)(2,1)S(1)} %bitcast.122), channel_id=1, source_target_pairs={{0,8},{8,0},{16,24},{24,16},{1,9},{9,1},{17,25},{25,17},{2,10},{10... | collective-permute-start | bytes 3145736 | tf_op jit(solution)/shard_map/ppermute | solution.py:16
  48.9 2.2 %copy-start.8 = (s32[512,8]{1,0:T(8,128)S(1)}, s32[512,8]{1,0:T(8,128)}, u32[]{:S(2)}) copy-start(s32[512,8]{1,0:T(8,128)} %iota_add_fusion) | copy-start | bytes 49156
  48.9 2.2 %copy-start.15 = (bf16[512,8,1]{1,2,0:T(2,128)(2,1)S(1)}, bf16[512,8,1]{1,2,0:T(2,128)(2,1)}, u32[]{:S(2)}) copy-start(bf16[512,8,1]{1,2,0:T(2,128)(2,1)} %copy.28) | copy-start | bytes 24580
  51.1 2.5 %copy-start.3 = (bf16[512,1,512]{2,0,1:T(8,128)(2,1)S(1)}, bf16[512,1,512]{2,0,1:T(8,128)(2,1)}, u32[]{:S(2)}) copy-start(bf16[512,1,512]{2,0,1:T(8,128)(2,1)} %copy.54) | copy-start | bytes 1572868
  51.2 2.5 %copy-start.4 = (bf16[512,512]{1,0:T(8,128)(2,1)S(1)}, bf16[512,512]{1,0:T(8,128)(2,1)}, u32[]{:S(2)}) copy-start(bf16[512,512]{1,0:T(8,128)(2,1)} %get-tuple-element.13) | copy-start | bytes 1572868
  51.2 2.5 %copy-start.5 = (bf16[512,512]{1,0:T(8,128)(2,1)S(1)}, bf16[512,512]{1,0:T(8,128)(2,1)}, u32[]{:S(2)}) copy-start(bf16[512,512]{1,0:T(8,128)(2,1)} %get-tuple-element.14) | copy-start | bytes 1572868
  53.6 15.4 %copy-start.6 = (bf16[512,512]{1,0:T(8,128)(2,1)S(1)}, bf16[512,512]{1,0:T(8,128)(2,1)}, u32[]{:S(2)}) copy-start(bf16[512,512]{1,0:T(8,128)(2,1)} %get-tuple-element.11) | copy-start | bytes 1572868
  53.6 15.4 %copy-start.7 = (bf16[512,512]{1,0:T(8,128)(2,1)S(1)}, bf16[512,512]{1,0:T(8,128)(2,1)}, u32[]{:S(2)}) copy-start(bf16[512,512]{1,0:T(8,128)(2,1)} %get-tuple-element.12) | copy-start | bytes 1572868
  72.5 47.6 %collective-permute-start.2 = (bf16[1024,512]{1,0:T(8,128)(2,1)}, bf16[1024,512]{1,0:T(8,128)(2,1)}, u32[]{:S(2)}, u32[]{:S(2)}) collective-permute-start(bf16[1024,512]{1,0:T(8,128)(2,1)} %add_convert_fusion.1), channel_id=1, source_target_pairs={{0,16},{8,24},{16,0},{24,8},{1,17},{9,25},{17,1},{25,9},{2,18},{10... | collective-permute-start | bytes 3145736 | tf_op jit(solution)/shard_map/ppermute | solution.py:16
  125.9 55.3 %all-to-all-start.1 = ((bf16[32,32,1024]{2,1,0:T(8,128)(2,1)}), bf16[32,32,1024]{2,1,0:T(8,128)(2,1)S(1)}, u32[]{:S(2)}, u32[]{:S(2)}) async-start(bf16[32,32,1024]{2,1,0:T(8,128)(2,1)} %bitcast.42), calls=%async_computation.1 | async-start | bytes 4194304 | tf_op jit(solution)/shard_map/all_to_all | solution.py:54
  (7 other events, 7.5 us)
where the time goes:
time: 185 us; the launch traced here: 183 us
  waiting for transfers between devices  100 us (54%)
  matrix products  34 us (18%)
  starting transfers between devices  20.8 us (11%)
  local copies, waits for them, and re-layouts  17.6 us (10%)
  other arithmetic  10.4 us (6%)
    ppermute x2, waiting for transfers between devices, from_partner(): lax.ppermute(value, axis, [(i, i ^ 1 << apart) for i in range(lax.axis_si...  53.7 us
    all_to_all x1, waiting for transfers between devices, route_rows(): lax.all_to_all(send, ('sub', 'rng'), split_axis=0, concat_axis=0, tiled=T...  46.3 us
    dot_general x4, matrix products, merge_matrix(): jnp.einsum('bk,bks->bs', kernel[0].astype(jnp.float32), hit)  9.16 us
    dot_general x4, matrix products, merge_matrix(): jnp.einsum('bk,bks->bs', kernel[1].astype(jnp.float32), hit)  8.93 us
    all_to_all x1, starting transfers between devices, route_rows(): lax.all_to_all(labels, ('sub', 'rng'), split_axis=0, concat_axis=0, tiled...  8.19 us
    all_to_all x1, starting transfers between devices, route_rows(): lax.all_to_all(send, ('sub', 'rng'), split_axis=0, concat_axis=0, tiled=T...  6.99 us
    dot_general x2, matrix products, on_device(): jnp.dot(theirs, partner, preferred_element_type=jnp.float32)  5.91 us
    dot_general x2, matrix products, on_device(): merged = jnp.dot(mine, image, preferred_element_type=jnp.float32)  3.7 us
  transfers between devices with their start and end apart: 5, of which 3 were waited for; matrix products, arithmetic and copies ran while one was open for 31% of the time, Pallas kernels for 0%

commit v1 on v0

v1 whole, which is shorter than its diff:
```python
import functools

import jax
import jax.numpy as jnp
from jax import lax
from jax.experimental import pallas as pl
from jax.experimental.pallas import tpu as pltpu
from jax.sharding import PartitionSpec as P

MESH = pl.DeviceIdType.MESH
BF = jnp.bfloat16
F32 = jnp.float32
CS = 64
CH = 128
NT = (((1,), (1,)), ((), ()))


def nt(a, b):
    return lax.dot_general(a, b, NT, preferred_element_type=F32)


def nn(a, b):
    return jnp.dot(a, b, preferred_element_type=F32)


def z_of(i, n_sub):
    return (i % 2) * (n_sub // 2) + i // 2


def kernel(
    n_sub, n_rng, sections, stages, cap,
    e_ref, chirp_ref, meta_ref, w_ref, out_ref,
    h_ref, tail, metas, wall, cmp, img, gt, ya, yb, pick, upper, labsend, lab, lrow, place, sbuf, got, tbuf,
    tail_s, tail_r, meta_s, meta_r, w_s, w_r, img_s, img_r, lab_s, lab_r, x_s, x_r, t_s, t_r, loc,
):
    z = lax.axis_index("sub")
    r = lax.axis_index("rng")
    p = e_ref.shape[1]
    rd_len = e_ref.shape[2]
    taps_len = rd_len
    chunks = rd_len // CH
    width = CH + taps_len
    keep = stages > 1
    dests = n_sub * n_rng

    barrier = pltpu.get_barrier_semaphore()
    for d in range(1, n_sub):
        pl.semaphore_signal(barrier, inc=1, device_id=(lax.rem(z + d, n_sub), r), device_id_type=MESH)
    for d in range(1, n_rng):
        pl.semaphore_signal(barrier, inc=1, device_id=(z, lax.rem(r + d, n_rng)), device_id_type=MESH)
    pl.semaphore_wait(barrier, n_sub + n_rng - 2)

    def remote(src, dst, ss, rs, dev):
        return pltpu.make_async_remote_copy(
            src_ref=src, dst_ref=dst, send_sem=ss, recv_sem=rs, device_id=dev, device_id_type=MESH
        )

    def tail_copy(k):
        span = pl.ds(k * CH, CH)
        left = jnp.where(r == 0, 1, r - 1)
        return remote(e_ref.at[:, :, span], tail.at[:, :, span], tail_s.at[k], tail_r.at[k], (z, left))

    @pl.when(r > 0)
    def _():
        for k in range(chunks):
            tail_copy(k).start()

    def meta_copy(src, d):
        peer = lax.rem(z + d, n_sub)
        return (
            remote(meta_ref, metas.at[src], meta_s.at[d], meta_r.at[src], (peer, r)),
            remote(w_ref, wall.at[src], w_s.at[d], w_r.at[src], (peer, r)),
        )

    for d in range(1, n_sub):
        for c in meta_copy(z, d):
            c.start()
    metas[z] = meta_ref[...]
    wall[z] = w_ref[...]

    @pl.when(r == n_rng - 1)
    def _():
        tail[...] = jnp.zeros_like(tail)

    parts = []
    for part in range(2):
        row = jnp.broadcast_to(chirp_ref[pl.ds(part, 1), :], (CH, width))
        parts.append(pltpu.roll(row, 0, 1, stride=1, stride_axis=0))
    h_re, h_im = parts
    h_ref[0, :CH] = h_re.astype(BF)
    h_ref[0, CH:] = (-h_im).astype(BF)
    h_ref[1, :CH] = h_im.astype(BF)
    h_ref[1, CH:] = h_re.astype(BF)

    def build_merge(section, g, slot):
        for side in range(2):
            j = section * 2 + side
            off = metas[g, pl.ds(j, 1), :]
            w = wall[g, j].astype(F32)
            spot = lax.broadcasted_iota(jnp.int32, (p, p), 0) - off
            hit = (spot >= 0) & (spot < 8)
            for part in range(2):
                wide = jnp.broadcast_to(w[part * 8 : part * 8 + 8][None], (p // 8, 8, p)).reshape(p, p)
                gt[slot, side, part] = jnp.where(hit, wide, 0.0).astype(BF)

    def build_pick(g, slot):
        owner = metas[g, pl.ds(6, 1), :]
        aim = metas[g, pl.ds(7, 1), :]
        onehot = jnp.where(lax.broadcasted_iota(jnp.int32, (dests, p), 0) == owner, 1.0, 0.0)
        before = nn(onehot.astype(BF), upper[...])
        rank = jnp.sum(onehot * before, axis=0, keepdims=True).astype(jnp.int32)
        zd = owner // n_rng
        where_to = ((owner - zd * n_rng) * n_sub + zd) * cap + rank
        hit = lax.broadcasted_iota(jnp.int32, (dests * cap, p), 0) == where_to
        pick[slot] = jnp.where(hit, 1.0, 0.0).astype(BF)
        mark = aim + 1
        hi = mark // 16
        lo = mark - hi * 16
        rows = lax.broadcasted_iota(jnp.int32, (16, p), 0)
        both = jnp.where(rows == 0, hi, jnp.where(rows == 1, lo, 0)).astype(F32).astype(BF)
        out = nt(both, pick[slot])
        label = out[0:1] * 16.0 + out[1:2] - 1.0
        for rd in range(n_rng):
            labsend[rd, pl.ds(g, 1), :] = label[:, rd * 128 : (rd + 1) * 128]

    before = lax.broadcasted_iota(jnp.int32, (p, p), 0) < lax.broadcasted_iota(jnp.int32, (p, p), 1)
    upper[...] = jnp.where(before, 1.0, 0.0).astype(BF)

    def img_copy(s, i, src):
        sub = s * n_sub + i
        k, o = sub // (CH // CS), sub % (CH // CS)
        view = cmp.at[k, :, pl.ds(o * CS, CS), :]
        zd = z_of(i, n_sub)
        return view, remote(view, img.at[s, src], img_s.at[s, i], img_r.at[s, src], (zd, r))

    def wait_meta(g):
        @pl.when(z != g)
        def _():
            for c in meta_copy(g, 1):
                c.wait_recv()

    for k in range(chunks):
        @pl.when(r < n_rng - 1)
        def _():
            tail_copy(k).wait_recv()

        cut = rd_len - CH * k
        acc = None
        for part in range(2):
            x = nt(h_ref[part, :, :cut], e_ref[part, :, CH * k :])
            y = nt(h_ref[part, :, cut:], tail[part, :, : CH * (k + 1)])
            acc = x + y if acc is None else acc + x + y
        cmp[k] = acc.astype(BF).reshape(2, CH, p)
        for o in range(CH // CS):
            sub = k * (CH // CS) + o
            s, i = sub // n_sub, sub % n_sub
            view, copy = img_copy(s, i, z)
            own = z == z_of(i, n_sub)

            @pl.when(own)
            def _():
                pltpu.make_async_copy(view, img.at[s, z], loc.at[s]).start()

            @pl.when(jnp.logical_not(own))
            def _():
                copy.start()

        if keep and k < n_sub:
            wait_meta(k)
            for section in range(sections):
                build_merge(section, k, section * n_sub + k)
            build_pick(k, k)

    for g in range(chunks if keep else 0, n_sub):
        wait_meta(g)
        if keep:
            for section in range(sections):
                build_merge(section, g, section * n_sub + g)
            build_pick(g, g)

    def lab_copy(src, d):
        peer = lax.rem(r + d, n_rng)
        return remote(labsend.at[peer], lab.at[src], lab_s.at[d], lab_r.at[src], (z, peer))

    def send_labels():
        for d in range(1, n_rng):
            lab_copy(r, d).start()
        lab[r] = labsend[r]

    def x_copy(s, src, d):
        peer = lax.rem(r + d, n_rng)
        return remote(sbuf.at[s, peer], got.at[s, :, src], x_s.at[s, d], x_r.at[s, src], (z, peer))

    def x_local(s):
        return pltpu.make_async_copy(sbuf.at[s, r], got.at[s, :, r], loc.at[stages + s])

    if keep:
        send_labels()

    for s in range(stages):
        pltpu.make_async_copy(img.at[s, z], img.at[s, z], loc.at[s]).wait()
        for d in range(1, n_sub):
            img_copy(s, 0, lax.rem(z + d, n_sub))[1].wait_recv()
        for section in range(sections):
            bit = 1 << section
            dst = (ya, yb)[section % 2]

            def load(g):
                if section == 0:
                    return img[s, g].reshape(2 * CS, p)
                return (ya, yb)[(section + 1) % 2][g]

            def merge(g, carry):
                q = g + bit - 2 * bit * ((g // bit) % 2)
                slot = section * n_sub + g
                if not keep:
                    slot = 0
                    build_merge(section, g, 0)
                own, other = load(g), load(q)
                a = nn(own, gt[slot, 0, 0]) + nn(other, gt[slot, 1, 0])
                b = nn(own, gt[slot, 0, 1]) + nn(other, gt[slot, 1, 1])
                dst[g, :CS] = (a[:CS] - b[CS:]).astype(BF)
                dst[g, CS:] = (a[CS:] + b[:CS]).astype(BF)
                return carry

            lax.fori_loop(0, n_sub, merge, 0)
        final = (ya, yb)[(sections - 1) % 2]

        def gather(g, carry):
            slot = g
            if not keep:
                slot = 0
                build_pick(g, 0)
            rows = nt(pick[slot], final[g]).astype(BF)
            sbuf[s, :, :, pl.ds(pl.multiple_of(g * cap, cap), cap), :] = rows.reshape(n_rng, n_sub, cap, 2 * CS)
            return carry

        lax.fori_loop(0, n_sub, gather, 0)
        for d in range(1, n_rng):
            x_copy(s, r, d).start()
        x_local(s).start()
        if not keep:
            send_labels()

    for d in range(1, n_rng):
        lab_copy(lax.rem(r + d, n_rng), d).wait_recv()
    lane = lax.broadcasted_iota(jnp.int32, (n_rng, 128), 1) // cap
    for zd in range(n_sub):
        total = jnp.zeros((n_rng, 128), F32)
        for g in range(n_sub):
            piece = lab[:, g, :]
            move = ((g - zd) * cap) % 128
            if move:
                piece = pltpu.roll(piece, move, 1)
            total = jnp.where(lane == g, piece, total)
        lrow[zd] = total

    def build_place(zd, slot):
        rows = lax.broadcasted_iota(jnp.int32, (p, 128), 0)
        for j in range(n_rng):
            label = lrow[zd, pl.ds(j, 1), :].astype(jnp.int32)
            place[slot, :, j * 128 : (j + 1) * 128] = jnp.where(rows == label, 1.0, 0.0).astype(BF)

    if keep:
        def run(zd, carry):
            build_place(zd, zd)
            return carry

        lax.fori_loop(0, n_sub, run, 0)

    def t_copy(s, src, zd, d):
        return remote(tbuf.at[s, zd], out_ref.at[s, src], t_s.at[s, d], t_r.at[s, src], (zd, r))

    for s in range(stages):
        x_local(s).wait()
        for d in range(1, n_rng):
            x_copy(s, lax.rem(r + d, n_rng), d).wait_recv()
        for d in list(range(1, n_sub)) + [0]:
            zd = lax.rem(z + d, n_sub)
            slot = zd
            if not keep:
                slot = 0
                build_place(zd, 0)
            tile = nn(place[slot], got[s, zd].reshape(n_rng * 128, 2 * CS)).astype(BF)
            if d:
                tbuf[s, zd] = tile
                t_copy(s, z, zd, d).start()
            else:
                out_ref[s, z] = tile

    for s in range(stages):
        for d in range(1, n_sub):
            peer = lax.rem(z + d, n_sub)
            t_copy(s, peer, peer, d).wait_recv()

    @pl.when(r > 0)
    def _():
        for k in range(chunks):
            tail_copy(k).wait_send()

    for d in range(1, n_sub):
        for c in meta_copy(z, d):
            c.wait_send()
    for s in range(stages):
        for i in range(n_sub):
            @pl.when(z != z_of(i, n_sub))
            def _():
                img_copy(s, i, z)[1].wait_send()

        for d in range(1, n_rng):
            x_copy(s, r, d).wait_send()
        for d in range(1, n_sub):
            t_copy(s, z, lax.rem(z + d, n_sub), d).wait_send()
    for d in range(1, n_rng):
        lab_copy(r, d).wait_send()


def on_device(echoes, chirp, offsets, weights, owners, targets):
    p = echoes.shape[1]
    r_dev = echoes.shape[2]
    n_sub = lax.axis_size("sub")
    n_rng = lax.axis_size("rng")
    devices = n_sub * n_rng
    sections = offsets.shape[0]
    cap = max(16, 2 * p // devices)
    stages = r_dev // (n_sub * CS)
    chunks = r_dev // CH
    keep = stages > 1

    off = offsets[:, 0]
    w = weights[:, 0].transpose(0, 1, 2, 4, 3)
    for bit in (1, 2, 4):
        w = jnp.where((off[:, :, None, None, :] & bit) != 0, jnp.roll(w, bit, axis=3), w)
    w = w.reshape(sections * 2, 16, p)
    meta = jnp.concatenate(
        [
            off.reshape(sections * 2, p),
            jnp.zeros((6 - sections * 2, p), jnp.int32),
            owners.reshape(1, p),
            targets.reshape(1, p),
        ]
    )
    taps = jnp.pad(chirp.astype(F32), ((0, 6), (0, CH)))

    vm = pltpu.VMEM
    dma = pltpu.SemaphoreType.DMA
    built = n_sub if keep else 1
    scratch = [
        vm((2, 2 * CH, CH + r_dev), BF),
        vm((2, p, r_dev), BF),
        vm((n_sub, 8, p), jnp.int32),
        vm((n_sub, sections * 2, 16, p), BF),
        vm((chunks, 2, CH, p), BF),
        vm((stages, n_sub, 2, CS, p), BF),
        vm((built * sections if keep else 1, 2, 2, p, p), BF),
        vm((n_sub, 2 * CS, p), BF),
        vm((n_sub, 2 * CS, p), BF),
        vm((built, devices * cap, p), BF),
        vm((p, p), BF),
        vm((n_rng, 8, 128), F32),
        vm((n_rng, 8, 128), F32),
        vm((n_sub, n_rng, 128), F32),
        vm((built, p, n_rng * 128), BF),
        vm((stages, n_rng, n_sub, n_sub * cap, 2 * CS), BF),
        vm((stages, n_sub, n_rng, n_sub * cap, 2 * CS), BF),
        vm((stages, n_sub, p, 2 * CS), BF),
        dma((chunks,)), dma((chunks,)),
        dma((n_sub,)), dma((n_sub,)),
        dma((n_sub,)), dma((n_sub,)),
        dma((stages, n_sub)), dma((stages, n_sub)),
        dma((n_rng,)), dma((n_rng,)),
        dma((stages, n_rng)), dma((stages, n_rng)),
        dma((stages, n_sub)), dma((stages, n_sub)),
        dma((2 * stages,)),
    ]
    out = pl.pallas_call(
        functools.partial(kernel, n_sub, n_rng, sections, stages, cap),
        out_shape=jax.ShapeDtypeStruct((stages, n_sub, p, 2 * CS), BF),
        in_specs=[pl.BlockSpec(memory_space=pltpu.VMEM)] * 4,
        out_specs=pl.BlockSpec(memory_space=pltpu.VMEM),
        scratch_shapes=scratch,
        compiler_params=pltpu.CompilerParams(
            collective_id=0, has_side_effects=True, vmem_limit_bytes=56 * 1024 * 1024
        ),
        cost_estimate=pl.CostEstimate(flops=8 * 10**9, bytes_accessed=4 * 10**6, transcendentals=0),
    )(echoes, taps, meta, w)
    half = n_sub // 2
    out = out.reshape(stages, 2, half, p, 2, CS).transpose(4, 3, 0, 2, 1, 5)
    return out.reshape(2, p, r_dev)


def solution(mesh):
    in_specs = (
        P(None, "sub", "rng"),
        P(),
        P(None, "sub", None, None),
        P(None, "sub", None, None, None, None),
        P("sub", "rng", None, None),
        P("sub", "rng", None),
    )
    out_specs = P(None, "sub", "rng")
    return jax.shard_map(
        on_device, mesh=mesh, in_specs=in_specs, out_specs=out_specs, check_vma=False
    )
```

time: 185 us -> 79.8 us (0.43)
  the two profiles are of different devices: /device:TPU:1 before, /device:TPU:13 now
where the time goes in v1:
time: 79.8 us; the launch traced here: 79.5 us
  Pallas kernels  71.5 us (90%)
  local copies, waits for them, and re-layouts  4.41 us (6%)
  other arithmetic  3.49 us (4%)
    pallas_call x1, Pallas kernels, on_device(): pl.pallas_call(functools.partial(kernel, n_sub, n_rng, sections, stages,...  71.5 us

profile of v1, /device:TPU:13, one launch (start us, length us, event | category | flops | bytes accessed | tf_op | source)
XLA Modules:
  0.0 79.5 jit_solution(8577931464072682464)
XLA Ops:
  0.0 0.0 copy-start
  0.0 0.1 pad.15.clone
  0.1 0.7 reshape_squeeze.3
  0.8 1.4 %pad_add_fusion.meta_ref = s32[8,512]{1,0:T(8,128)} fusion(s32[1,512]{1,0:T(1,128)} %bitcast.25, s32[1,512]{1,0:T(1,128)} %bitcast.26, s32[4,512]{1,0:T(4,128)S(1)} %reshape_squeeze.3, s32[8]{0:T(128)S(1)} %pad.15.clone), kind=kLoop, calls=%fused_computation.3 | loop fusion | flops 12288 | bytes 28704 | tf_op jit(solution)/shard_map/concatenate | solution.py:335
  2.2 0.7 compare_bitcast_fusion.2
  2.9 0.0 copy-done
  2.9 0.0 copy-start.1
  2.9 0.6 copy-done.1
  3.6 0.6 pad_convert_fusion.chirp_ref
  4.2 0.1 maximum_select_fusion
  4.3 0.1 maximum_select_fusion.1
  4.4 0.7 maximum_select_fusion.2
  5.1 71.5 %shard_map.64 = bf16[2,4,512,128]{3,2,1,0:T(8,128)(2,1)} custom-call(bf16[2,512,512]{2,1,0:T(8,128)(2,1)} %e_ref.1, f32[8,640]{1,0:T(8,128)} %pad_convert_fusion.chirp_ref, s32[8,512]{1,0:T(8,128)} %pad_add_fusion.meta_ref, bf16[4,16,512]{2,1,0:T(8,128)(2,1)} %bitcast.24), custom_call_target="tpu_custom_call" | custom-call | flops 8000000000 | bytes 4000000 | tf_op jit(solution)/shard_map/pallas_call | solution.py:376
  76.6 1.5 %copy.8 = bf16[2,4,512,128]{2,3,1,0:T(8,128)(2,1)S(1)} copy(bf16[2,4,512,128]{3,2,1,0:T(8,128)(2,1)} %shard_map.64) | data formatting | bytes 2097152 | tf_op jit(solution)/shard_map/pallas_call | solution.py:376
  78.1 0.1 copy.9
  78.2 1.3 %copy.10 = bf16[2,512,512]{2,1,0:T(8,128)(2,1)} copy(bf16[2,512,512]{1,2,0:T(8,128)(2,1)S(1)} %bitcast.20) | data formatting | bytes 2097152 | tf_op jit(solution)/shard_map/reshape | solution.py:389
  (4 shorter events, 0.1 us)
Async XLA Ops:
  0.0 2.9 %copy-start = (bf16[2,1,2,2,512,8]{4,5,3,2,1,0:T(8,128)(2,1)S(1)}, bf16[2,1,2,2,512,8]{4,5,3,2,1,0:T(8,128)(2,1)}, u32[]{:S(2)}) copy-start(bf16[2,1,2,2,512,8]{4,5,3,2,1,0:T(8,128)(2,1)} %param.9) | copy-start | bytes 196612
  2.9 0.7 copy-start.1

commit v2 on v1

--- a/solution.py
+++ b/solution.py
@@ -29,8 +29,8 @@
 
 def kernel(
     n_sub, n_rng, sections, stages, cap,
-    e_ref, chirp_ref, meta_ref, w_ref, out_ref,
-    h_ref, tail, metas, wall, cmp, img, gt, ya, yb, pick, upper, labsend, lab, lrow, place, sbuf, got, tbuf,
+    e_ref, chirp_ref, off_ref, own_ref, aim_ref, w_ref, out_ref,
+    h_ref, tail, metas, wall, cmp, img, gt, ya, yb, pick, upper, labsend, lab, lrow, place, sbuf, got, tbuf, obuf,
     tail_s, tail_r, meta_s, meta_r, w_s, w_r, img_s, img_r, lab_s, lab_r, x_s, x_r, t_s, t_r, loc,
 ):
     z = lax.axis_index("sub")
@@ -48,49 +48,66 @@
         pl.semaphore_signal(barrier, inc=1, device_id=(lax.rem(z + d, n_sub), r), device_id_type=MESH)
     for d in range(1, n_rng):
         pl.semaphore_signal(barrier, inc=1, device_id=(z, lax.rem(r + d, n_rng)), device_id_type=MESH)
-    pl.semaphore_wait(barrier, n_sub + n_rng - 2)
-
-    def remote(src, dst, ss, rs, dev):
-        return pltpu.make_async_remote_copy(
-            src_ref=src, dst_ref=dst, send_sem=ss, recv_sem=rs, device_id=dev, device_id_type=MESH
-        )
-
-    def tail_copy(k):
-        span = pl.ds(k * CH, CH)
-        left = jnp.where(r == 0, 1, r - 1)
-        return remote(e_ref.at[:, :, span], tail.at[:, :, span], tail_s.at[k], tail_r.at[k], (z, left))
-
-    @pl.when(r > 0)
-    def _():
-        for k in range(chunks):
-            tail_copy(k).start()
-
-    def meta_copy(src, d):
-        peer = lax.rem(z + d, n_sub)
-        return (
-            remote(meta_ref, metas.at[src], meta_s.at[d], meta_r.at[src], (peer, r)),
-            remote(w_ref, wall.at[src], w_s.at[d], w_r.at[src], (peer, r)),
-        )
-
-    for d in range(1, n_sub):
-        for c in meta_copy(z, d):
-            c.start()
-    metas[z] = meta_ref[...]
-    wall[z] = w_ref[...]
-
-    @pl.when(r == n_rng - 1)
-    def _():
-        tail[...] = jnp.zeros_like(tail)
-
+
+    taps = chirp_ref[...].astype(F32)
     parts = []
     for part in range(2):
-        row = jnp.broadcast_to(chirp_ref[pl.ds(part, 1), :], (CH, width))
-        parts.append(pltpu.roll(row, 0, 1, stride=1, stride_axis=0))
+        row = jnp.concatenate([taps[part : part + 1], jnp.zeros((1, CH), F32)], axis=1)
+        parts.append(pltpu.roll(jnp.broadcast_to(row, (CH, width)), 0, 1, stride=1, stride_axis=0))
     h_re, h_im = parts
     h_ref[0, :CH] = h_re.astype(BF)
     h_ref[0, CH:] = (-h_im).astype(BF)
     h_ref[1, :CH] = h_im.astype(BF)
     h_ref[1, CH:] = h_re.astype(BF)
+
+    for section in range(sections):
+        for side in range(2):
+            j = section * 2 + side
+            off = off_ref[section, pl.ds(side, 1), :]
+            both = []
+            for part in range(2):
+                w = w_ref[j * 2 + part].astype(F32)
+                for bit in (1, 2, 4):
+                    odd = jnp.broadcast_to((off // bit) % 2, (8, p)) == 1
+                    w = jnp.where(odd, pltpu.roll(w, bit, 0), w)
+                both.append(w)
+            wall[z, j] = jnp.concatenate(both, axis=0).astype(BF)
+            metas[z, pl.ds(j, 1), :] = off
+    metas[z, pl.ds(6, 1), :] = own_ref[...]
+    metas[z, pl.ds(7, 1), :] = aim_ref[...]
+    for j in range(sections * 2, 6):
+        metas[z, pl.ds(j, 1), :] = jnp.zeros((1, p), jnp.int32)
+    pl.semaphore_wait(barrier, n_sub + n_rng - 2)
+
+    def remote(src, dst, ss, rs, dev):
+        return pltpu.make_async_remote_copy(
+            src_ref=src, dst_ref=dst, send_sem=ss, recv_sem=rs, device_id=dev, device_id_type=MESH
+        )
+
+    def tail_copy(k):
+        span = pl.ds(k * CH, CH)
+        left = jnp.where(r == 0, 1, r - 1)
+        return remote(e_ref.at[:, :, span], tail.at[:, :, span], tail_s.at[k], tail_r.at[k], (z, left))
+
+    @pl.when(r > 0)
+    def _():
+        for k in range(chunks):
+            tail_copy(k).start()
+
+    def meta_copy(src, d):
+        peer = lax.rem(z + d, n_sub)
+        return (
+            remote(metas.at[z], metas.at[src], meta_s.at[d], meta_r.at[src], (peer, r)),
+            remote(wall.at[z], wall.at[src], w_s.at[d], w_r.at[src], (peer, r)),
+        )
+
+    for d in range(1, n_sub):
+        for c in meta_copy(z, d):
+            c.start()
+
+    @pl.when(r == n_rng - 1)
+    def _():
+        tail[...] = jnp.zeros_like(tail)
 
     def build_merge(section, g, slot):
         for side in range(2):
@@ -199,8 +216,6 @@
 
     for s in range(stages):
         pltpu.make_async_copy(img.at[s, z], img.at[s, z], loc.at[s]).wait()
-        for d in range(1, n_sub):
-            img_copy(s, 0, lax.rem(z + d, n_sub))[1].wait_recv()
         for section in range(sections):
             bit = 1 << section
             dst = (ya, yb)[section % 2]
@@ -223,7 +238,17 @@
                 dst[g, CS:] = (a[CS:] + b[:CS]).astype(BF)
                 return carry
 
-            lax.fori_loop(0, n_sub, merge, 0)
+            if section == 0:
+                for away in range(n_sub // 2):
+                    pair = lax.rem(z // 2 + away, n_sub // 2)
+                    if away == 0:
+                        img_copy(s, 0, z + 1 - 2 * (z % 2))[1].wait_recv()
+                    else:
+                        img_copy(s, 0, 2 * pair)[1].wait_recv()
+                        img_copy(s, 0, 2 * pair + 1)[1].wait_recv()
+                    lax.fori_loop(2 * pair, 2 * pair + 2, merge, 0)
+            else:
+                lax.fori_loop(0, n_sub, merge, 0)
         final = (ya, yb)[(sections - 1) % 2]
 
         def gather(g, carry):
@@ -269,7 +294,7 @@
         lax.fori_loop(0, n_sub, run, 0)
 
     def t_copy(s, src, zd, d):
-        return remote(tbuf.at[s, zd], out_ref.at[s, src], t_s.at[s, d], t_r.at[s, src], (zd, r))
+        return remote(tbuf.at[s, zd], obuf.at[s, src], t_s.at[s, d], t_r.at[s, src], (zd, r))
 
     for s in range(stages):
         x_local(s).wait()
@@ -286,12 +311,17 @@
                 tbuf[s, zd] = tile
                 t_copy(s, z, zd, d).start()
             else:
-                out_ref[s, z] = tile
+                obuf[s, z] = tile
 
     for s in range(stages):
         for d in range(1, n_sub):
             peer = lax.rem(z + d, n_sub)
             t_copy(s, peer, peer, d).wait_recv()
+        for i in range(0, n_sub, 2):
+            low, high = obuf[s, z_of(i, n_sub)], obuf[s, z_of(i + 1, n_sub)]
+            span = slice((s * n_sub + i) * CS, (s * n_sub + i + 2) * CS)
+            out_ref[0, :, span] = jnp.concatenate([low[:, :CS], high[:, :CS]], axis=1)
+            out_ref[1, :, span] = jnp.concatenate([low[:, CS:], high[:, CS:]], axis=1)
 
     @pl.when(r > 0)
     def _():
@@ -326,22 +356,6 @@
     stages = r_dev // (n_sub * CS)
     chunks = r_dev // CH
     keep = stages > 1
-
-    off = offsets[:, 0]
-    w = weights[:, 0].transpose(0, 1, 2, 4, 3)
-    for bit in (1, 2, 4):
-        w = jnp.where((off[:, :, None, None, :] & bit) != 0, jnp.roll(w, bit, axis=3), w)
-    w = w.reshape(sections * 2, 16, p)
-    meta = jnp.concatenate(
-        [
-            off.reshape(sections * 2, p),
-            jnp.zeros((6 - sections * 2, p), jnp.int32),
-            owners.reshape(1, p),
-            targets.reshape(1, p),
-        ]
-    )
-    taps = jnp.pad(chirp.astype(F32), ((0, 6), (0, CH)))
-
     vm = pltpu.VMEM
     dma = pltpu.SemaphoreType.DMA
     built = n_sub if keep else 1
@@ -364,6 +378,7 @@
         vm((stages, n_rng, n_sub, n_sub * cap, 2 * CS), BF),
         vm((stages, n_sub, n_rng, n_sub * cap, 2 * CS), BF),
         vm((stages, n_sub, p, 2 * CS), BF),
+        vm((stages, n_sub, p, 2 * CS), BF),
         dma((chunks,)), dma((chunks,)),
         dma((n_sub,)), dma((n_sub,)),
         dma((n_sub,)), dma((n_sub,)),
@@ -373,20 +388,24 @@
         dma((stages, n_sub)), dma((stages, n_sub)),
         dma((2 * stages,)),
     ]
-    out = pl.pallas_call(
+    return pl.pallas_call(
         functools.partial(kernel, n_sub, n_rng, sections, stages, cap),
-        out_shape=jax.ShapeDtypeStruct((stages, n_sub, p, 2 * CS), BF),
-        in_specs=[pl.BlockSpec(memory_space=pltpu.VMEM)] * 4,
+        out_shape=jax.ShapeDtypeStruct((2, p, r_dev), BF),
+        in_specs=[pl.BlockSpec(memory_space=pltpu.VMEM)] * 6,
         out_specs=pl.BlockSpec(memory_space=pltpu.VMEM),
         scratch_shapes=scratch,
         compiler_params=pltpu.CompilerParams(
             collective_id=0, has_side_effects=True, vmem_limit_bytes=56 * 1024 * 1024
         ),
         cost_estimate=pl.CostEstimate(flops=8 * 10**9, bytes_accessed=4 * 10**6, transcendentals=0),
-    )(echoes, taps, meta, w)
-    half = n_sub // 2
-    out = out.reshape(stages, 2, half, p, 2, CS).transpose(4, 3, 0, 2, 1, 5)
-    return out.reshape(2, p, r_dev)
+    )(
+        echoes,
+        chirp,
+        offsets[:, 0],
+        owners.reshape(1, p),
+        targets.reshape(1, p),
+        weights.transpose(0, 1, 2, 3, 5, 4).reshape(sections * 4, weights.shape[-1], p),
+    )
 
 
 def solution(mesh):

time: 79.8 us -> 73.9 us (0.926)
  the two profiles are of different devices: /device:TPU:13 before, /device:TPU:1 now
where the time goes in v2:
time: 73.9 us; the launch traced here: 73.7 us
  Pallas kernels  71.5 us (97%)
  local copies, waits for them, and re-layouts  2.26 us (3%)
    pallas_call x1, Pallas kernels, on_device(): pl.pallas_call(functools.partial(kernel, n_sub, n_rng, sections, stages,...  71.5 us
    unnamed x1, local copies, waits for them, and re-layouts  2.26 us

profile of v2, /device:TPU:1, one launch (start us, length us, event | category | flops | bytes accessed | tf_op | source)
XLA Modules:
  0.0 73.7 jit_solution(820037096909738310)
XLA Ops:
  0.0 71.5 %shard_map.64 = bf16[2,512,512]{2,1,0:T(8,128)(2,1)} custom-call(bf16[2,512,512]{2,1,0:T(8,128)(2,1)} %e_ref.1, bf16[2,512]{1,0:T(2,128)(2,1)} %chirp_ref.1, s32[2,2,512]{2,1,0:T(2,128)} %bitcast.7, s32[1,512]{1,0:T(1,128)} %bitcast.8, s32[1,512]{1,0:T(1,128)} %bitcast.9, bf16[8,8,512]{2,1,0:T(8,128)(2,1)} %bitcast.6), custom_call_target="tpu_custom_call" | custom-call | flops 8000000000 | bytes 4000000 | tf_op jit(solution)/shard_map/pallas_call | solution.py:391
  71.5 2.3 %copy.8 = bf16[2,512,512]{2,1,0:T(8,128)(2,1)} copy(bf16[2,512,512]{2,1,0:T(8,128)(2,1)} %shard_map.64) | data formatting | bytes 2097152

commit v3 on v2

--- a/solution.py
+++ b/solution.py
@@ -118,7 +118,7 @@
             hit = (spot >= 0) & (spot < 8)
             for part in range(2):
                 wide = jnp.broadcast_to(w[part * 8 : part * 8 + 8][None], (p // 8, 8, p)).reshape(p, p)
-                gt[slot, side, part] = jnp.where(hit, wide, 0.0).astype(BF)
+                gt[slot, side * p : side * p + p, part * p : part * p + p] = jnp.where(hit, wide, 0.0).astype(BF)
 
     def build_pick(g, slot):
         owner = metas[g, pl.ds(6, 1), :]
@@ -184,14 +184,13 @@
 
         if keep and k < n_sub:
             wait_meta(k)
-            for section in range(sections):
-                build_merge(section, k, section * n_sub + k)
-            build_pick(k, k)
-
-    for g in range(chunks if keep else 0, n_sub):
-        wait_meta(g)
+            build_merge(0, k, k)
+
+    for g in range(n_sub):
+        if not keep or g >= chunks:
+            wait_meta(g)
         if keep:
-            for section in range(sections):
+            for section in range(1 if g < chunks else 0, sections):
                 build_merge(section, g, section * n_sub + g)
             build_pick(g, g)
 
@@ -231,9 +230,8 @@
                 if not keep:
                     slot = 0
                     build_merge(section, g, 0)
-                own, other = load(g), load(q)
-                a = nn(own, gt[slot, 0, 0]) + nn(other, gt[slot, 1, 0])
-                b = nn(own, gt[slot, 0, 1]) + nn(other, gt[slot, 1, 1])
+                both = nn(jnp.concatenate([load(g), load(q)], axis=1), gt[slot])
+                a, b = both[:, :p], both[:, p:]
                 dst[g, :CS] = (a[:CS] - b[CS:]).astype(BF)
                 dst[g, CS:] = (a[CS:] + b[:CS]).astype(BF)
                 return carry
@@ -293,6 +291,13 @@
 
         lax.fori_loop(0, n_sub, run, 0)
 
+    def flip(bits):
+        at = z
+        for j in range(bits.bit_length()):
+            if bits >> j & 1:
+                at = at + (1 << j) - (2 << j) * ((z // (1 << j)) % 2)
+        return at
+
     def t_copy(s, src, zd, d):
         return remote(tbuf.at[s, zd], obuf.at[s, src], t_s.at[s, d], t_r.at[s, src], (zd, r))
 
@@ -300,8 +305,8 @@
         x_local(s).wait()
         for d in range(1, n_rng):
             x_copy(s, lax.rem(r + d, n_rng), d).wait_recv()
-        for d in list(range(1, n_sub)) + [0]:
-            zd = lax.rem(z + d, n_sub)
+        for d in range(n_sub - 1, -1, -1):
+            zd = flip(d)
             slot = zd
             if not keep:
                 slot = 0
@@ -340,7 +345,7 @@
         for d in range(1, n_rng):
             x_copy(s, r, d).wait_send()
         for d in range(1, n_sub):
-            t_copy(s, z, lax.rem(z + d, n_sub), d).wait_send()
+            t_copy(s, z, flip(d), d).wait_send()
     for d in range(1, n_rng):
         lab_copy(r, d).wait_send()
 
@@ -366,7 +371,7 @@
         vm((n_sub, sections * 2, 16, p), BF),
         vm((chunks, 2, CH, p), BF),
         vm((stages, n_sub, 2, CS, p), BF),
-        vm((built * sections if keep else 1, 2, 2, p, p), BF),
+        vm((built * sections if keep else 1, 2 * p, 2 * p), BF),
         vm((n_sub, 2 * CS, p), BF),
         vm((n_sub, 2 * CS, p), BF),
         vm((built, devices * cap, p), BF),

time: 73.9 us -> 75.2 us (1.018)
  Pallas kernels: 71.5 us -> 72.7 us
    pallas_call x1, Pallas kernels: 71.5 us -> 72.7 us  [on_device(): pl.pallas_call(functools.partial(kernel, n_sub, n_rng, sections, stages,...]
where the time goes in v3:
time: 75.2 us; the launch traced here: 75 us
  Pallas kernels  72.7 us (97%)
  local copies, waits for them, and re-layouts  2.26 us (3%)
    pallas_call x1, Pallas kernels, on_device(): pl.pallas_call(functools.partial(kernel, n_sub, n_rng, sections, stages,...  72.7 us
    unnamed x1, local copies, waits for them, and re-layouts  2.26 us

profile of v3, /device:TPU:1, one launch (start us, length us, event | category | flops | bytes accessed | tf_op | source)
XLA Modules:
  0.0 75.0 jit_solution(289317258880358364)
XLA Ops:
  0.0 72.7 %shard_map.64 = bf16[2,512,512]{2,1,0:T(8,128)(2,1)} custom-call(bf16[2,512,512]{2,1,0:T(8,128)(2,1)} %e_ref.1, bf16[2,512]{1,0:T(2,128)(2,1)} %chirp_ref.1, s32[2,2,512]{2,1,0:T(2,128)} %bitcast.7, s32[1,512]{1,0:T(1,128)} %bitcast.8, s32[1,512]{1,0:T(1,128)} %bitcast.9, bf16[8,8,512]{2,1,0:T(8,128)(2,1)} %bitcast.6), custom_call_target="tpu_custom_call" | custom-call | flops 8000000000 | bytes 4000000 | tf_op jit(solution)/shard_map/pallas_call | solution.py:396
  72.7 2.3 %copy.8 = bf16[2,512,512]{2,1,0:T(8,128)(2,1)} copy(bf16[2,512,512]{2,1,0:T(8,128)(2,1)} %shard_map.64) | data formatting | bytes 2097152
